TPU v7x, 768 devices: a whole 4x8x12 slice. The times are simulated.
768 devices in a mesh: dp: 96 (over x, z_lo, y), tensor: 8 (over z_hi, core).
Axes of the slice: x: 4, y: 8, z: 12 (z_hi: 4, z_lo: 3; z = z_hi * 3 + z_lo), core: 2. Of those that a mesh axis runs over, the one named last changes fastest.
Arguments:
- decode_states: bfloat16 [12288, 12288], P('dp'), may hold values from -6 to 6
- query_weight: float32 [12288, 1024], P('dp', 'tensor'), may hold values from -0.3125 to 0.3125
- query_exponents: int32 [96, 8], P('dp', 'tensor'), may hold values from -16 to -13
- output_weight: float32 [1024, 12288], P('tensor', 'dp'), may hold values from -0.4375 to 0.4375
- output_exponents: int32 [8, 96], P('tensor', 'dp'), may hold values from -15 to -12
Outputs:
- mixed: bfloat16 [12288, 12288], P('dp', 'tensor')
All inputs are finite; a program needn't handle non-finite values.
Results may differ from a plain program's by a relative error of at most 0.017.
Values may be sent and summed in bfloat16 or wider, within the bound.
A program may use at most 32 MiB of HBM per device.

v0:
```python
import jax
import jax.numpy as jnp
from jax import lax
from jax.sharding import PartitionSpec as P


def block_scales(exponents):
    power = exponents.astype(jnp.float32)
    inverse = lax.optimization_barrier(jnp.exp2(-power).astype(jnp.bfloat16)).astype(jnp.float32)
    scales = jnp.exp2(power).astype(jnp.bfloat16)
    return (inverse, scales)


def quantize_rows(weight, exponents, block):
    inverse, scales = block_scales(exponents)
    row_count, col_count = weight.shape
    shaped = weight.reshape(row_count // block, block, col_count // block, block)
    codes = jnp.clip(shaped * inverse[:, None, :, None], -448.0, 448.0).astype(jnp.bfloat16)
    return (codes.reshape(row_count, col_count), scales)


def dequant_query(codes, row_scales, block):
    row_count, col_count = codes.shape
    shaped = codes.reshape(row_count, col_count // block, block) * row_scales[:, :, None]
    return shaped.reshape(row_count, col_count)


def dequant_output(codes, col_scales, block):
    row_count, col_count = codes.shape
    shaped = codes.reshape(row_count // block, block, col_count) * col_scales[:, None, :]
    return shaped.reshape(row_count, col_count)


def per_device(decode_states, query_weight, query_exponents, output_weight, output_exponents):
    block = query_weight.shape[0] // query_exponents.shape[0]
    query_codes, query_scales = quantize_rows(query_weight, query_exponents, block)
    query_row_scales = jnp.repeat(query_scales, block, axis=0)
    output_codes, output_scales = quantize_rows(output_weight, output_exponents, block)
    output_col_scales = jnp.repeat(output_scales, block, axis=1)
    gathered_codes, gathered_scales = (
        lax.all_gather(query_codes, "dp", axis=0, tiled=True),
        lax.all_gather(query_row_scales, "dp", axis=0, tiled=True),
    )
    dense = dequant_query(gathered_codes, gathered_scales, block)
    queries = jnp.dot(decode_states, dense, preferred_element_type=jnp.float32)
    queries = queries.astype(jnp.bfloat16)
    pieces = lax.all_gather((output_codes, output_col_scales), "dp", axis=1, tiled=True)
    dense = dequant_output(pieces[0], pieces[1], block)
    partial_value = jnp.dot(queries, dense, preferred_element_type=jnp.float32)
    whole = lax.psum(partial_value.astype(jnp.bfloat16), "tensor").astype(jnp.float32)
    share_width = whole.shape[1] // lax.axis_size("tensor")
    summed = lax.dynamic_slice_in_dim(whole, lax.axis_index("tensor") * share_width, share_width, 1)
    return summed.astype(jnp.bfloat16)


def solution(mesh):
    return jax.shard_map(
        per_device,
        mesh=mesh,
        in_specs=(
            P("dp", None),
            P("dp", "tensor"),
            P("dp", "tensor"),
            P("tensor", "dp"),
            P("tensor", "dp"),
        ),
        out_specs=P("dp", "tensor"),
        check_vma=False,
    )
```

profile of v0, /device:TPU:1, one launch (start us, length us, event | category | flops | bytes accessed | tf_op | source)
XLA Modules:
  0.0 1125.7 jit_solution(18118320820047908747)
XLA Ops:
  6.5 0.0 copy-start
  6.5 0.0 all-gather.5.cloned.1.call-start
  7.4 1.6 clamp_convert_fusion
  9.0 0.0 all-gather.5.cloned.1.call-update
  9.0 0.0 all-gather.3.cloned.1.call-start
  9.7 1.5 clamp_convert_fusion.1
  11.2 0.0 all-gather.3.cloned.1.call-update
  11.2 0.0 all-reduce.2.cloned.1.call-start
  11.4 214.3 %all_gather.15 = bf16[1,12288]{1,0:T(2,128)(2,1)S(1)} all-gather(bf16[1,128]{1,0:T(2,128)(2,1)S(1)} %reshape.43), channel_id=1, replica_groups=mesh['dp'=96,'tensor'=8] {'dp'}, dimensions={1}, use_global_device_ids=true | all-gather | bytes 24832 | tf_op jit(solution)/shard_map/all_gather | solution.py:47
  225.6 0.1 reduce.1
  225.8 203.9 %all_gather.13 = bf16[12288,1]{0,1:T(2,128)(2,1)S(1)} all-gather(bf16[128,1]{0,1:T(2,128)(2,1)S(1)} %reshape.42), channel_id=1, replica_groups=mesh['dp'=96,'tensor'=8] {'dp'}, dimensions={0}, use_global_device_ids=true | all-gather | bytes 24832 | tf_op jit(solution)/shard_map/all_gather | solution.py:42
  429.6 0.1 reduce
  429.8 0.0 all-gather.5.cloned.1.call-done
  429.8 430.4 %all-gather.3.cloned.1.call-done = bf16[12288,128]{1,0:T(8,128)(2,1)} async-done(((bf16[128,128]{1,0:T(8,128)(2,1)}), bf16[12288,128]{1,0:T(8,128)(2,1)}) %all-gather.3.cloned.1.call-update) | async-done | bytes 3145744 | tf_op jit(solution)/shard_map/all_gather | solution.py:41
  860.2 0.0 copy-done
  860.2 10.1 convolution_convert_fusion
  870.3 0.0 all-reduce.2.cloned.1.call-update
  870.4 247.0 %all-reduce.2.cloned.1.call-done = bf16[128,12288]{1,0:T(8,128)(2,1)} async-done(((bf16[128,12288]{1,0:T(8,128)(2,1)}), bf16[128,12288]{1,0:T(8,128)(2,1)}) %all-reduce.2.cloned.1.call-update) | async-done | bytes 3145744 | tf_op jit(solution)/shard_map/psum | solution.py:50
  1117.4 1.8 convert_convert_fusion
  (2 shorter events, 0.0 us)
Async XLA Ops:
  6.5 853.7 %copy-start = (bf16[128,12288]{1,0:T(8,128)(2,1)S(1)}, bf16[128,12288]{1,0:T(8,128)(2,1)}, u32[]{:S(2)}) copy-start(bf16[128,12288]{1,0:T(8,128)(2,1)} %param.5) | copy-start | bytes 9437188
  6.5 423.2 %all-gather.5.cloned.1.call-start = ((), (), s32[]{:S(2)}) async-start(), calls=%async_computation.1 | async-start | bytes 3178496 | tf_op jit(solution)/shard_map/all_gather | solution.py:47
  9.0 851.2 %all-gather.3.cloned.1.call-start = ((), (), s32[]{:S(2)}) async-start(), calls=%async_computation | async-start | bytes 3178496 | tf_op jit(solution)/shard_map/all_gather | solution.py:41
  11.2 1106.2 %all-reduce.2.cloned.1.call-start = ((), (), s32[]{:S(2)}) async-start(), calls=%async_computation.2 | async-start | bytes 6291456 | tf_op jit(solution)/shard_map/psum | solution.py:50
Sparse Core Ops, SparseCore 0:
  9.7 337.7 all-gather.4
  349.9 510.2 all-gather.2
  870.5 246.8 all-reduce.1
where the time goes:
time: 1130 us
  waiting for transfers between devices  678 us (60%)
  blocking collectives  418 us (37%)
  between operations  14.8 us (1%)
    all_gather x1, waiting for transfers between devices, per_device(): lax.all_gather(query_codes, 'dp', axis=0, tiled=True)  430 us
    psum x1, waiting for transfers between devices, per_device(): lax.psum(partial_value.astype(jnp.bfloat16), 'tensor').astype(jnp.float32)  247 us
    all_gather x1, blocking collectives, per_device(): lax.all_gather((output_codes, output_col_scales), 'dp', axis=1, tiled=True)  214 us
    all_gather x1, blocking collectives, per_device(): lax.all_gather(query_row_scales, 'dp', axis=0, tiled=True)  204 us
  transfers between devices with their start and end apart: 3, of which 2 were waited for; matrix products, arithmetic and copies ran while one was open for 0% of the time, Pallas kernels for 0%

commit v1 on v0

v1 whole, which is shorter than its diff:
```python
import functools

import jax
import jax.numpy as jnp
from jax import lax
from jax.experimental import pallas as pl
from jax.experimental.pallas import tpu as pltpu
from jax.sharding import PartitionSpec as P

MESH = pl.DeviceIdType.MESH
NX, NY, NZ, NH = 4, 8, 3, 4
BLK = 128
HALF = NZ * NY // 2


def device(x, y, zl, zh, c):
    return ((x * NZ + zl) * NY + y, zh * 2 + c)


def ring_order(n):
    return jnp.where(n % 2 == 1, (n + 1) // 2, (NY - n // 2) % NY)


def dense_block(weight_ref, exponent_ref):
    power = exponent_ref[...].astype(jnp.float32)
    inverse = jnp.exp2(-power).astype(jnp.bfloat16).astype(jnp.float32)
    scale = jnp.exp2(power).astype(jnp.bfloat16).astype(jnp.float32)
    codes = jnp.clip(weight_ref[...] * inverse, -448.0, 448.0).astype(jnp.bfloat16)
    return (codes.astype(jnp.float32) * scale).astype(jnp.bfloat16)


def kernel(x_hbm, qw_ref, qe_ref, ow_ref, oe_ref, out_ref,
           xv, wq, wo, wos, qacc, qcat, acc, pout, pin,
           x_sem, wq_send, wq_recv, wo_send, wo_recv, a_send, b_send, q_send, q_recv, p_send, p_recv):
    d = lax.axis_index("dp")
    t = lax.axis_index("tensor")
    y = d % NY
    zl = (d // NY) % NZ
    x = d // (NY * NZ)
    zh = t // 2
    c = t % 2
    collector = x == zh

    def at(dx=0, dy=0, dz=0, dh=0, dc=0):
        return device((x + dx) % NX, (y + dy) % NY, (zl + dz) % NZ, (zh + dh) % NH, (c + dc) % 2)

    x_copy = pltpu.make_async_copy(x_hbm, xv, x_sem)
    x_copy.start()

    barrier = pltpu.get_barrier_semaphore()
    partners = [at(dy=k) for k in range(1, NY)] + [at(dz=k) for k in range(1, NZ)]
    partners += [at(dx=k) for k in range(1, NX)] + [at(dh=k) for k in range(1, NH)] + [at(dc=1)]
    for partner in partners:
        pl.semaphore_signal(barrier, inc=1, device_id=partner, device_id_type=MESH)

    def qi(dx, dz, dy):
        return (((x + dx) % NX) * NZ + (zl + dz) % NZ) * NY + (y + dy) % NY

    def oi(dz, dy, h):
        return (((zl + dz) % NZ) * NY + (y + dy) % NY) * NH + h

    own_q = qi(0, 0, 0)
    own_o = oi(0, 0, zh)
    wq[own_q] = dense_block(qw_ref, qe_ref)
    wos[...] = dense_block(ow_ref, oe_ref)

    @pl.when(collector)
    def _():
        wo[own_o] = wos[...]

    pl.semaphore_wait(barrier, len(partners))

    def q_copy(b, to):
        return pltpu.make_async_remote_copy(wq.at[b], wq.at[b], wq_send, wq_recv.at[b], device_id=to, device_id_type=MESH)

    def o_copy(b, to, sem):
        return pltpu.make_async_remote_copy(wo.at[b], wo.at[b], sem, wo_recv.at[b], device_id=to, device_id_type=MESH)

    def q_wait(b):
        q_copy(b, at(dx=1)).wait_recv()

    def o_wait(b):
        o_copy(b, at(dx=1), wo_send).wait_recv()

    def a_copy():
        to = device(x, y, zl, x, c)
        return pltpu.make_async_remote_copy(wos, wo.at[own_o], a_send, wo_recv.at[own_o], device_id=to, device_id_type=MESH)

    @pl.when(jnp.logical_not(collector))
    def _():
        a_copy().start()

    q_copy(own_q, at(dx=1)).start()
    q_copy(own_q, at(dx=3)).start()
    for k in (1, 7, 2, 6, 3, 5, 4):
        q_copy(own_q, at(dy=k)).start()
    for k in (1, 2):
        q_copy(own_q, at(dz=k)).start()

    @pl.loop(1, NY)
    def _(n):
        b = qi(0, 0, ring_order(n))
        q_wait(b)
        q_copy(b, at(dx=1)).start()
        q_copy(b, at(dx=3)).start()
        q_copy(b, at(dz=1)).start()
        q_copy(b, at(dz=2)).start()

    def o_spread(b):
        o_copy(b, at(dy=1), wo_send).start()
        o_copy(b, at(dy=7), wo_send).start()

    def o_first(b):
        o_spread(b)
        o_copy(b, at(dz=1), wo_send).start()
        o_copy(b, at(dz=2), wo_send).start()

    @pl.when(collector)
    def _():
        @pl.loop(0, NH)
        def _(i):
            b = oi(0, 0, (zh + i) % NH)

            @pl.when(i > 0)
            def _():
                o_wait(b)

            for k in (1, 3, 2):
                o_copy(b, at(dx=k), b_send).start()
            o_first(b)

    @pl.loop(0, NY)
    def _(n):
        for dz in (1, 2):
            b = qi(0, dz, ring_order(n))
            q_wait(b)
            q_copy(b, at(dx=1)).start()
            q_copy(b, at(dx=3)).start()

    @pl.when(jnp.logical_not(collector))
    def _():
        @pl.loop(0, NH)
        def _(i):
            b = oi(0, 0, (zh + i) % NH)
            o_wait(b)
            o_first(b)

    @pl.loop(0, NH)
    def _(i):
        for dz in (1, 2):
            b = oi(dz, 0, (zh + i) % NH)
            o_wait(b)
            o_spread(b)

    def q_forward(m):
        late = m - NY
        dz = jnp.where(m < NY, 0, 1 + late % 2)
        dy = ring_order(jnp.where(m < NY, m, late // 2))
        even = ((y + dy) % NY) % 2 == 0
        left = qi(3, dz, dy)
        right = qi(1, dz, dy)
        q_wait(left)

        @pl.when(even)
        def _():
            q_copy(left, at(dx=1)).start()

        q_wait(right)

        @pl.when(jnp.logical_not(even))
        def _():
            q_copy(right, at(dx=3)).start()

    @pl.loop(0, NZ * NY)
    def _(m):
        q_forward(m)
        k = 1 + m // 12
        r = m % 12
        h = (zh + r % NH) % NH
        left = oi(r // NH, NY - k, h)
        right = oi(r // NH, k, h)
        o_wait(left)
        o_copy(left, at(dy=1), wo_send).start()
        o_wait(right)
        o_copy(right, at(dy=7), wo_send).start()

    x_copy.wait()
    qacc[...] = jnp.zeros_like(qacc)

    def q_dot(chunk):
        columns = pl.ds(pl.multiple_of(chunk * (NY * BLK), NY * BLK), NY * BLK)
        w = wq[pl.ds(chunk * NY, NY)].reshape(NY * BLK, BLK)
        qacc[...] += jnp.dot(xv[:, columns], w, preferred_element_type=jnp.float32)

    @pl.loop(0, 12)
    def _(r):
        h = (zh + r % NH) % NH
        left = oi(r // NH, NY - 3, h)
        right = oi(r // NH, 3, h)
        o_wait(left)

        @pl.when(h < 2)
        def _():
            o_copy(left, at(dy=1), wo_send).start()

        o_wait(right)

        @pl.when(h >= 2)
        def _():
            o_copy(right, at(dy=7), wo_send).start()

        @pl.when(r < 9)
        def _():
            plane = r // 3
            dx = jnp.where(plane == 0, 0, jnp.where(plane == 1, 3, 1))
            q_dot(((x + dx) % NX) * NZ + r % NZ)

    @pl.loop(0, NZ)
    def _(dz):
        @pl.loop(0, NY)
        def _(n):
            q_wait(qi(2, dz, ring_order(n)))

        q_dot(((x + 2) % NX) * NZ + (zl + dz) % NZ)

    own_cols = qcat.at[:, pl.ds(pl.multiple_of(zh * BLK, BLK), BLK)]
    own_cols[...] = qacc[...].astype(jnp.bfloat16)

    def x_query(k):
        return pltpu.make_async_remote_copy(
            own_cols, own_cols, q_send.at[k], q_recv.at[zh], device_id=at(dh=k), device_id_type=MESH)

    for k in (2, 1, 3):
        x_query(k).start()

    @pl.loop(0, 12)
    def _(r):
        o_wait(oi(r // NH, 4, r % NH))

    for k in (1, 2, 3):
        h = (zh + k) % NH
        cols = qcat.at[:, pl.ds(pl.multiple_of(h * BLK, BLK), BLK)]
        pltpu.make_async_remote_copy(cols, cols, q_send.at[k], q_recv.at[h], device_id=at(dh=k), device_id_type=MESH).wait_recv()

    def half_sum(j):
        w = wo[pl.ds(j * NH, NH)].reshape(NH * BLK, BLK)
        return jnp.dot(qcat[...], w, preferred_element_type=jnp.float32)

    def p_copy(j):
        return pltpu.make_async_remote_copy(pout.at[j], pin.at[j], p_send.at[j], p_recv.at[j], device_id=at(dc=1), device_id_type=MESH)

    @pl.loop(0, HALF)
    def _(j):
        pout[j] = half_sum((1 - c) * HALF + j).astype(jnp.bfloat16)
        p_copy(j).start()

    @pl.loop(0, HALF)
    def _(j):
        acc[j] = half_sum(c * HALF + j)

    for j in range(HALF):
        p_copy(j).wait_recv()
        out_ref[:, j * BLK:(j + 1) * BLK] = (acc[j] + pin[j].astype(jnp.float32)).astype(jnp.bfloat16)

    for j in range(HALF):
        p_copy(j).wait_send()
    for k in (1, 2, 3):
        x_query(k).wait_send()
    sent = wq.at[pl.ds(0, 95)]
    pltpu.make_async_remote_copy(sent, sent, wq_send, wq_recv.at[0], device_id=at(dx=1), device_id_type=MESH).wait_send()
    sent = wo.at[pl.ds(0, 92)]
    pltpu.make_async_remote_copy(sent, sent, wo_send, wo_recv.at[0], device_id=at(dx=1), device_id_type=MESH).wait_send()

    @pl.when(collector)
    def _():
        some = wo.at[pl.ds(0, 12)]
        pltpu.make_async_remote_copy(some, some, b_send, wo_recv.at[0], device_id=at(dx=1), device_id_type=MESH).wait_send()

    @pl.when(jnp.logical_not(collector))
    def _():
        a_copy().wait_send()


def per_device(decode_states, query_weight, query_exponents, output_weight, output_exponents):
    rows, width = decode_states.shape
    vmem = pl.BlockSpec(memory_space=pltpu.VMEM)
    bf16, f32 = jnp.bfloat16, jnp.float32
    dma = pltpu.SemaphoreType.DMA
    return pl.pallas_call(
        kernel,
        out_shape=jax.ShapeDtypeStruct((rows, HALF * BLK), bf16),
        in_specs=[pl.BlockSpec(memory_space=pl.ANY), vmem, vmem, vmem, vmem],
        out_specs=vmem,
        scratch_shapes=[
            pltpu.VMEM((rows, width), bf16),
            pltpu.VMEM((96, BLK, BLK), bf16),
            pltpu.VMEM((96, BLK, BLK), bf16),
            pltpu.VMEM((BLK, BLK), bf16),
            pltpu.VMEM((rows, BLK), f32),
            pltpu.VMEM((rows, NH * BLK), bf16),
            pltpu.VMEM((HALF, BLK, BLK), f32),
            pltpu.VMEM((HALF, BLK, BLK), bf16),
            pltpu.VMEM((HALF, BLK, BLK), bf16),
            dma, dma, dma((96,)), dma, dma((96,)), dma, dma, dma((NH,)), dma((NH,)), dma((HALF,)), dma((HALF,)),
        ],
        compiler_params=pltpu.CompilerParams(collective_id=0, has_side_effects=True, vmem_limit_bytes=48 << 20),
        cost_estimate=pl.CostEstimate(flops=805306368, bytes_accessed=4 << 20, transcendentals=0),
    )(decode_states, query_weight, query_exponents, output_weight, output_exponents)


def solution(mesh):
    return jax.shard_map(
        per_device,
        mesh=mesh,
        in_specs=(
            P("dp", None),
            P("dp", "tensor"),
            P("dp", "tensor"),
            P("tensor", "dp"),
            P("tensor", "dp"),
        ),
        out_specs=P("dp", "tensor"),
        check_vma=False,
    )
```

time: 1130 us -> 82 us (0.07)
  waiting for transfers between devices: 678 us -> 0 us
  blocking collectives: 418 us -> 0 us
  Pallas kernels: 0 us -> 75.8 us
  between operations: 14.8 us -> 1.32 us
    all_gather x2 -> x0, waiting for transfers between devices: 430 us -> none  [the longest x1 430 us: per_device(): lax.all_gather(query_codes, 'dp', axis=0, tiled=True)]
    all_gather x2 -> x0, blocking collectives: 418 us -> none  [the longest x1 214 us: per_device(): lax.all_gather((output_codes, output_col_scales), 'dp', axis=1, tiled=True)]
    psum x1 -> x0, waiting for transfers between devices: 247 us -> none  [per_device(): lax.psum(partial_value.astype(jnp.bfloat16), 'tensor').astype(jnp.float32)]
    pallas_call x0 -> x1, Pallas kernels: none -> 75.8 us  [per_device(): pl.pallas_call(kernel, out_shape=jax.ShapeDtypeStruct((rows, HALF * BLK),...]
  transfers between devices with their start and end apart: 3 -> 0, of which waited for: 2 -> 0; matrix products, arithmetic and copies ran while one was open for 0% -> 0% of each run, Pallas kernels for 0% -> 0%
where the time goes in v1:
time: 82 us; the launch traced here: 81.4 us
  Pallas kernels  75.8 us (92%)
  local copies, waits for them, and re-layouts  4.31 us (5%)
  between operations  1.32 us (2%)
    pallas_call x1, Pallas kernels, per_device(): pl.pallas_call(kernel, out_shape=jax.ShapeDtypeStruct((rows, HALF * BLK),...  75.8 us
    unnamed x7, local copies, waits for them, and re-layouts  4.31 us

profile of v1, /device:TPU:1, one launch (start us, length us, event | category | flops | bytes accessed | tf_op | source)
XLA Modules:
  0.0 81.4 jit_solution(18015367002286447775)
XLA Ops:
  1.3 0.0 copy-start
  1.3 1.9 %copy-done = bf16[128,12288]{1,0:T(8,128)(2,1)S(1)} copy-done((bf16[128,12288]{1,0:T(8,128)(2,1)S(1)}, bf16[128,12288]{1,0:T(8,128)(2,1)}, u32[]{:S(2)}) %copy-start) | copy-done | bytes 3145752
  3.2 0.0 copy-start.1
  3.2 0.8 %copy-done.1 = f32[128,128]{1,0:T(8,128)S(1)} copy-done((f32[128,128]{1,0:T(8,128)S(1)}, f32[128,128]{1,0:T(8,128)}, u32[]{:S(2)}) %copy-start.1) | copy-done | bytes 65560
  4.0 0.0 copy-start.2
  4.0 0.8 %copy-done.2 = f32[128,128]{1,0:T(8,128)S(1)} copy-done((f32[128,128]{1,0:T(8,128)S(1)}, f32[128,128]{1,0:T(8,128)}, u32[]{:S(2)}) %copy-start.2) | copy-done | bytes 65560
  4.9 75.8 %shard_map.55 = bf16[128,1536]{1,0:T(8,128)(2,1)S(1)} custom-call(bf16[128,12288]{1,0:T(8,128)(2,1)S(1)} %copy-done, f32[128,128]{1,0:T(8,128)S(1)} %copy-done.1, s32[1,1]{1,0:T(1,128)S(6)} %copy.7.qe_ref, f32[128,128]{1,0:T(8,128)S(1)} %copy-done.2, s32[1,1]{1,0:T(1,128)S(6)} %copy.8.oe_ref), custom_call_target="tpu_custom_call" | custom-call | flops 805306368 | bytes 4194304 | tf_op jit(solution)/shard_map/pallas_call | solution.py:289
  80.7 0.7 copy.9
Async XLA Ops:
  1.3 1.9 %copy-start = (bf16[128,12288]{1,0:T(8,128)(2,1)S(1)}, bf16[128,12288]{1,0:T(8,128)(2,1)}, u32[]{:S(2)}) copy-start(bf16[128,12288]{1,0:T(8,128)(2,1)} %x_hbm.1) | copy-start | bytes 9437188
  3.2 0.8 %copy-start.1 = (f32[128,128]{1,0:T(8,128)S(1)}, f32[128,128]{1,0:T(8,128)}, u32[]{:S(2)}) copy-start(f32[128,128]{1,0:T(8,128)} %qw_ref.1) | copy-start | bytes 196612
  4.0 0.8 %copy-start.2 = (f32[128,128]{1,0:T(8,128)S(1)}, f32[128,128]{1,0:T(8,128)}, u32[]{:S(2)}) copy-start(f32[128,128]{1,0:T(8,128)} %ow_ref.1) | copy-start | bytes 196612

commit v2 on v0

v2 whole, which is shorter than its diff:
```python
import functools

import jax
import jax.numpy as jnp
from jax import lax
from jax.experimental import pallas as pl
from jax.experimental.pallas import tpu as pltpu
from jax.sharding import PartitionSpec as P

MESH = pl.DeviceIdType.MESH
NX, NY, NZ, NH = 4, 8, 3, 4
BLK = 128
HALF = NZ * NY // 2
VMEM_LIMIT = 61 << 20


def device(x, y, zl, zh, c):
    return ((x * NZ + zl) * NY + y, zh * 2 + c)


def dense_block(weight_ref, exponent_ref):
    power = exponent_ref[...].astype(jnp.float32)
    inverse = jnp.exp2(-power).astype(jnp.bfloat16).astype(jnp.float32)
    scale = jnp.exp2(power).astype(jnp.bfloat16).astype(jnp.float32)
    codes = jnp.clip(weight_ref[...] * inverse, -448.0, 448.0).astype(jnp.bfloat16)
    return (codes.astype(jnp.float32) * scale).astype(jnp.bfloat16)


def kernel(x_hbm, qw_hbm, qe_ref, ow_hbm, oe_ref, out_ref,
           xv, qw_ref, ow_ref, wq, wqs, wo, wos, qacc, qown, qcat, pout, pin,
           x_sem, w_sems, own_send, wq_send, wq_recv, wo_send, wo_recv, a_send, b_send, q_send, q_recv, p_send, p_recv):
    d = lax.axis_index("dp")
    t = lax.axis_index("tensor")
    y = d % NY
    zl = (d // NY) % NZ
    x = d // (NY * NZ)
    zh = t // 2
    c = t % 2
    collector = x == zh

    def on(core, dx=0, dy=0, dz=0, dh=0):
        return device((x + dx) % NX, (y + dy) % NY, (zl + dz) % NZ, (zh + dh) % NH, core)

    def copy(src, dst, send, recv, to):
        return pltpu.make_async_remote_copy(src, dst, send, recv, device_id=to, device_id_type=MESH)

    qw_copy = pltpu.make_async_copy(qw_hbm, qw_ref, w_sems.at[0])
    ow_copy = pltpu.make_async_copy(ow_hbm, ow_ref, w_sems.at[1])
    x_copy = pltpu.make_async_copy(x_hbm, xv, x_sem)
    qw_copy.start()
    ow_copy.start()

    barrier = pltpu.get_barrier_semaphore()
    near = [dict(dx=1), dict(dx=3), dict(dy=1), dict(dy=7), dict(dz=1), dict(dz=2)]
    heads = [dict(dh=2), dict(dh=1), dict(dh=3)]

    def greet(core, where):
        pl.semaphore_signal(barrier, inc=1, device_id=on(core, **where), device_id_type=MESH)

    @pl.when(c == 0)
    def _():
        x_copy.start()
        for where in near:
            greet(0, where)
        for where in [{}] + near:
            greet(1, where)

    @pl.when(c == 1)
    def _():
        for where in heads:
            greet(1, where)
            greet(0, where)
        for where in [dict(dx=2)] + near:
            greet(1, where)
        greet(0, {})

    def qi(dx, dz, dy):
        return (((x + dx) % NX) * NZ + (zl + dz) % NZ) * NY + (y + dy) % NY

    def oi(dz, dy, h):
        return (((zl + dz) % NZ) * NY + (y + dy) % NY) * NH + h

    own_q = qi(0, 0, 0)
    own_o = oi(0, 0, zh)
    qw_copy.wait()
    wqs[...] = dense_block(qw_ref, qe_ref)
    ow_copy.wait()
    wos[...] = dense_block(ow_ref, oe_ref)

    def q_half(b):
        return wq.at[b, :, pl.ds(pl.multiple_of(c * BLK, BLK), BLK)]

    def o_half(b):
        return wo.at[b, pl.ds(pl.multiple_of(c * BLK, BLK), BLK)]

    def own_copy(to):
        return copy(wqs, q_half(own_q), own_send, wq_recv.at[own_q], to)

    def a_copy():
        return copy(wos, o_half(own_o), a_send, wo_recv.at[own_o], device(x, y, zl, x, 1))

    def q_copy(b, to):
        return copy(wq.at[b], wq.at[b], wq_send, wq_recv.at[b], to)

    def q_wait(b):
        q_copy(b, on(0, dx=1)).wait_recv()

    def o_copy(b, to, sem):
        return copy(wo.at[b], wo.at[b], sem, wo_recv.at[b], to)

    def o_wait(b):
        o_copy(b, on(1, dy=1), wo_send).wait_recv()

    def x_query(k):
        cols = qcat.at[:, pl.ds(pl.multiple_of(zh * 2 * BLK, 2 * BLK), 2 * BLK)]
        return copy(qown, cols, q_send.at[k], q_recv.at[zh], on(1, dh=k))

    def p_copy(j, core):
        return copy(pout.at[j], pin.at[j], p_send.at[j], p_recv.at[j], on(core))

    def sent(ref, sem):
        copy(ref, ref, sem, wo_recv.at[0], on(1 - c)).wait_send()

    def query_core():
        half = q_half(own_q)
        half[...] = wqs[...]
        pl.semaphore_wait(barrier, 10)
        a_copy().start()
        for where in (dict(dz=1), dict(dz=2), dict(dy=1), dict(dy=7), dict(dx=1), dict(dx=3)):
            own_copy(on(0, **where)).start()

        def planes(b):
            q_copy(b, on(0, dx=1)).start()
            q_copy(b, on(0, dx=3)).start()

        for dz in (1, 2):
            b = qi(0, dz, 0)
            q_wait(b)
            q_copy(b, on(0, dy=1)).start()
            q_copy(b, on(0, dy=7)).start()
            planes(b)

        @pl.loop(0, 9)
        def _(n):
            k = 1 + n // NZ
            dz = n % NZ
            left, right = qi(0, dz, NY - k), qi(0, dz, k)
            even = ((zl + dz) % NZ + y + k) % 2 == 0
            q_wait(left)

            @pl.when(jnp.logical_or(k < 3, even))
            def _():
                q_copy(left, on(0, dy=1)).start()

            planes(left)
            q_wait(right)

            @pl.when(jnp.logical_or(k < 3, jnp.logical_not(even)))
            def _():
                q_copy(right, on(0, dy=7)).start()

            planes(right)

        @pl.loop(0, NZ)
        def _(dz):
            b = qi(0, dz, 4)
            q_wait(b)
            planes(b)

        own = q_half(own_q)
        copy(own, own, wq_send, wq_recv.at[own_q], on(1)).wait_recv()
        x_copy.wait()
        qacc[...] = jnp.zeros_like(qacc)

        def q_dot(dx, dz):
            chunk = ((x + dx) % NX) * NZ + (zl + dz) % NZ
            columns = pl.ds(pl.multiple_of(chunk * (NY * BLK), NY * BLK), NY * BLK)
            w = wq[pl.ds(chunk * NY, NY)].reshape(NY * BLK, 2 * BLK)
            qacc[...] += jnp.dot(xv[:, columns], w, preferred_element_type=jnp.float32)

        @pl.loop(0, NZ * NY)
        def _(m):
            r = jnp.maximum(m - NZ, 0)
            k = jnp.where(m < NZ, 0, 1 + r // 6)
            dz = jnp.where(m < NZ, m, jnp.where(r < 18, (r % 6) // 2, r - 18))
            dy = jnp.where(r % 2 == 0, NY - k, k)
            even = ((y + dy) % NY) % 2 == 0
            left = qi(3, dz, dy)
            right = qi(1, dz, dy)
            q_wait(left)

            @pl.when(even)
            def _():
                q_copy(left, on(0, dx=1)).start()

            q_wait(right)

            @pl.when(jnp.logical_not(even))
            def _():
                q_copy(right, on(0, dx=3)).start()

            @pl.when(m % 8 == 4)
            def _():
                q_dot(0, m // 8)

        @pl.loop(0, 6)
        def _(m):
            q_dot(3 - 2 * (m % 2), m // 2)

        @pl.loop(0, NZ)
        def _(dz):
            @pl.loop(0, NY)
            def _(n):
                q_wait(qi(2, dz, n))

            q_dot(2, dz)

        qown[...] = qacc[...].astype(jnp.bfloat16)
        for k in (2, 1, 3, 0):
            x_query(k).start()

        for j in range(HALF):
            p_copy(j, 1).wait_recv()
            out_ref[:, j * BLK:(j + 1) * BLK] = pin[j]

        for k in range(NH):
            x_query(k).wait_send()
        sent(wq.at[pl.ds(0, 89)], wq_send)
        sent(pin.at[pl.ds(0, 6)], own_send)
        sent(wos, a_send)

    def output_core():
        @pl.when(collector)
        def _():
            half = o_half(own_o)
            half[...] = wos[...]

        pl.semaphore_wait(barrier, 17)

        @pl.when(jnp.logical_not(collector))
        def _():
            a_copy().start()

        for where in (dict(dz=1), dict(dz=2), dict(dy=1), dict(dy=7), dict(dx=1), dict(dx=3), {}):
            own_copy(on(0, **where)).start()

        def group(i):
            return (zh + jnp.where(i == 2, 3, jnp.where(i == 3, 2, i))) % NH

        def spread(b):
            o_copy(b, on(1, dy=1), wo_send).start()
            o_copy(b, on(1, dy=7), wo_send).start()

        def lanes(b):
            o_copy(b, on(1, dz=1), wo_send).start()
            o_copy(b, on(1, dz=2), wo_send).start()

        @pl.loop(0, NH)
        def _(i):
            b = oi(0, 0, group(i))
            mine = jnp.logical_and(collector, i == 0)

            @pl.when(mine)
            def _():
                other = wo.at[own_o, pl.ds(0, BLK)]
                copy(other, other, wo_send, wo_recv.at[own_o], on(0)).wait_recv()

            @pl.when(jnp.logical_not(mine))
            def _():
                o_wait(b)

            @pl.when(collector)
            def _():
                for k in (2, 1, 3):
                    o_copy(b, on(1, dx=k), b_send).start()

            spread(b)
            lanes(b)

        @pl.loop(0, NH - 1)
        def _(i):
            for dz in (1, 2):
                b = oi(dz, 0, group(i))
                o_wait(b)
                spread(b)

        def ring(r, k):
            i = jnp.where(r == 0, NH - 1, lax.rem(r + 2, 3))
            dz = jnp.where(r == 0, 0, (r - 1) // 3)
            h = group(i)
            even = ((zl + dz) % NZ + h + (y + k)) % 2 == 0
            return oi(dz, NY - k, h), oi(dz, k, h), even

        @pl.loop(0, 30)
        def _(m):
            r = m % 10
            k = 1 + m // 10
            left, right, even = ring(r, k)
            o_wait(left)

            @pl.when(jnp.logical_or(k < 3, even))
            def _():
                o_copy(left, on(1, dy=1), wo_send).start()

            o_wait(right)

            @pl.when(jnp.logical_or(k < 3, jnp.logical_not(even)))
            def _():
                o_copy(right, on(1, dy=7), wo_send).start()

            @pl.when(r == 0)
            def _():
                lanes(left)
                lanes(right)

        @pl.loop(0, 10)
        def _(r):
            last, _, _ = ring(r, 4)
            o_wait(last)

            @pl.when(r == 0)
            def _():
                lanes(last)

        @pl.loop(0, NY)
        def _(n):
            for dz in (1, 2):
                o_wait(oi(dz, n, group(NH - 1)))

        for k in range(NH):
            h = (zh + k) % NH
            cols = qcat.at[:, pl.ds(pl.multiple_of(h * 2 * BLK, 2 * BLK), 2 * BLK)]
            copy(cols, cols, q_send.at[k], q_recv.at[h], on(0, dh=k)).wait_recv()

        def whole_sum(j):
            w = wo[pl.ds(j * NH, NH)].reshape(NH * 2 * BLK, BLK)
            return jnp.dot(qcat[...], w, preferred_element_type=jnp.float32).astype(jnp.bfloat16)

        @pl.loop(0, HALF)
        def _(j):
            pout[j] = whole_sum(j)
            p_copy(j, 0).start()

        for j in range(HALF):
            out_ref[:, j * BLK:(j + 1) * BLK] = whole_sum(HALF + j)

        for j in range(HALF):
            p_copy(j, 0).wait_send()
        sent(wo.at[pl.ds(0, 92)], wo_send)
        sent(pin.at[pl.ds(0, 7)], own_send)

        @pl.when(collector)
        def _():
            sent(wo.at[pl.ds(0, 12)], b_send)

        @pl.when(jnp.logical_not(collector))
        def _():
            sent(wos, a_send)

    pl.when(c == 0)(query_core)
    pl.when(c == 1)(output_core)


def per_device(decode_states, query_weight, query_exponents, output_weight, output_exponents):
    rows, width = decode_states.shape
    vmem = pl.BlockSpec(memory_space=pltpu.VMEM)
    hbm = pl.BlockSpec(memory_space=pltpu.HBM)
    bf16, f32 = jnp.bfloat16, jnp.float32
    dma = pltpu.SemaphoreType.DMA
    return pl.pallas_call(
        kernel,
        out_shape=jax.ShapeDtypeStruct((rows, HALF * BLK), bf16),
        in_specs=[hbm, hbm, vmem, hbm, vmem],
        out_specs=vmem,
        scratch_shapes=[
            pltpu.VMEM((rows, width), bf16),
            pltpu.VMEM((BLK, BLK), f32),
            pltpu.VMEM((BLK, BLK), f32),
            pltpu.VMEM((96, BLK, 2 * BLK), bf16),
            pltpu.VMEM((BLK, BLK), bf16),
            pltpu.VMEM((96, 2 * BLK, BLK), bf16),
            pltpu.VMEM((BLK, BLK), bf16),
            pltpu.VMEM((rows, 2 * BLK), f32),
            pltpu.VMEM((rows, 2 * BLK), bf16),
            pltpu.VMEM((rows, 2 * NH * BLK), bf16),
            pltpu.VMEM((HALF, BLK, BLK), bf16),
            pltpu.VMEM((HALF, BLK, BLK), bf16),
            dma, dma((2,)), dma, dma, dma((96,)), dma, dma((96,)), dma, dma, dma((NH,)), dma((NH,)), dma((HALF,)), dma((HALF,)),
        ],
        compiler_params=pltpu.CompilerParams(collective_id=0, has_side_effects=True, vmem_limit_bytes=VMEM_LIMIT),
        cost_estimate=pl.CostEstimate(flops=805306368, bytes_accessed=4 << 20, transcendentals=0),
    )(decode_states, query_weight, query_exponents, output_weight, output_exponents)


def solution(mesh):
    return jax.shard_map(
        per_device,
        mesh=mesh,
        in_specs=(
            P("dp", None),
            P("dp", "tensor"),
            P("dp", "tensor"),
            P("tensor", "dp"),
            P("tensor", "dp"),
        ),
        out_specs=P("dp", "tensor"),
        check_vma=False,
    )
```

time: 1130 us -> 70 us (0.06)
  waiting for transfers between devices: 678 us -> 0 us
  blocking collectives: 418 us -> 0 us
  Pallas kernels: 0 us -> 66.6 us
  between operations: 14.8 us -> 1.3 us
    all_gather x2 -> x0, waiting for transfers between devices: 430 us -> none  [the longest x1 430 us: per_device(): lax.all_gather(query_codes, 'dp', axis=0, tiled=True)]
    all_gather x2 -> x0, blocking collectives: 418 us -> none  [the longest x1 214 us: per_device(): lax.all_gather((output_codes, output_col_scales), 'dp', axis=1, tiled=True)]
    psum x1 -> x0, waiting for transfers between devices: 247 us -> none  [per_device(): lax.psum(partial_value.astype(jnp.bfloat16), 'tensor').astype(jnp.float32)]
    pallas_call x0 -> x1, Pallas kernels: none -> 66.6 us  [per_device(): pl.pallas_call(kernel, out_shape=jax.ShapeDtypeStruct((rows, HALF * BLK),...]
  transfers between devices with their start and end apart: 3 -> 0, of which waited for: 2 -> 0; matrix products, arithmetic and copies ran while one was open for 0% -> 0% of each run, Pallas kernels for 0% -> 0%
where the time goes in v2:
time: 70 us; the launch traced here: 69.7 us
  Pallas kernels  66.6 us (95%)
  local copies, waits for them, and re-layouts  1.77 us (3%)
  between operations  1.3 us (2%)
    pallas_call x1, Pallas kernels, per_device(): pl.pallas_call(kernel, out_shape=jax.ShapeDtypeStruct((rows, HALF * BLK),...  66.6 us
    unnamed x1, local copies, waits for them, and re-layouts  1.77 us

profile of v2, /device:TPU:1, one launch (start us, length us, event | category | flops | bytes accessed | tf_op | source)
XLA Modules:
  0.0 69.7 jit_solution(14403463786152607379)
XLA Ops:
  1.3 66.6 %shard_map.55 = bf16[128,1536]{1,0:T(8,128)(2,1)} custom-call(bf16[128,12288]{1,0:T(8,128)(2,1)} %x_hbm.1, f32[128,128]{1,0:T(8,128)} %qw_hbm.1, s32[1,1]{1,0:T(1,128)S(6)} %copy.7.qe_ref, f32[128,128]{1,0:T(8,128)} %ow_hbm.1, s32[1,1]{1,0:T(1,128)S(6)} %copy.8.oe_ref), custom_call_target="tpu_custom_call" | custom-call | flops 805306368 | bytes 4194304 | tf_op jit(solution)/shard_map/pallas_call | solution.py:370
  67.9 1.8 %copy.9 = bf16[128,1536]{1,0:T(8,128)(2,1)} copy(bf16[128,1536]{1,0:T(8,128)(2,1)} %shard_map.55) | data formatting | bytes 786432

commit v3 on v2

--- a/solution.py
+++ b/solution.py
@@ -37,6 +37,7 @@
     zh = t // 2
     c = t % 2
     collector = x == zh
+    behind = (x + NX - zh) % NX
 
     def on(core, dx=0, dy=0, dz=0, dh=0):
         return device((x + dx) % NX, (y + dy) % NY, (zl + dz) % NZ, (zh + dh) % NH, core)
@@ -70,7 +71,7 @@
         for where in heads:
             greet(1, where)
             greet(0, where)
-        for where in [dict(dx=2)] + near:
+        for where in near:
             greet(1, where)
         greet(0, {})
 
@@ -140,6 +141,28 @@
             q_copy(b, on(0, dy=7)).start()
             planes(b)
 
+        def crossing(left, right, even):
+            q_wait(left)
+
+            @pl.when(even)
+            def _():
+                q_copy(left, on(0, dx=1)).start()
+
+            q_wait(right)
+
+            @pl.when(jnp.logical_not(even))
+            def _():
+                q_copy(right, on(0, dx=3)).start()
+
+        def opposite(dy):
+            crossing(qi(3, 0, dy), qi(1, 0, dy), (zl + y + dy) % 2 == 0)
+
+        def lanes(dy):
+            b = qi(2, 0, dy)
+            q_wait(b)
+            q_copy(b, on(0, dz=1)).start()
+            q_copy(b, on(0, dz=2)).start()
+
         @pl.loop(0, 9)
         def _(n):
             k = 1 + n // NZ
@@ -161,6 +184,21 @@
 
             planes(right)
 
+            @pl.when(n == 2)
+            def _():
+                opposite(0)
+
+            @pl.when(n == 5)
+            def _():
+                opposite(1)
+                opposite(7)
+                lanes(0)
+
+            @pl.when(n == 8)
+            def _():
+                lanes(1)
+                lanes(7)
+
         @pl.loop(0, NZ)
         def _(dz):
             b = qi(0, dz, 4)
@@ -172,48 +210,44 @@
         x_copy.wait()
         qacc[...] = jnp.zeros_like(qacc)
 
-        def q_dot(dx, dz):
-            chunk = ((x + dx) % NX) * NZ + (zl + dz) % NZ
-            columns = pl.ds(pl.multiple_of(chunk * (NY * BLK), NY * BLK), NY * BLK)
-            w = wq[pl.ds(chunk * NY, NY)].reshape(NY * BLK, 2 * BLK)
-            qacc[...] += jnp.dot(xv[:, columns], w, preferred_element_type=jnp.float32)
-
-        @pl.loop(0, NZ * NY)
-        def _(m):
+        def place(m):
             r = jnp.maximum(m - NZ, 0)
             k = jnp.where(m < NZ, 0, 1 + r // 6)
             dz = jnp.where(m < NZ, m, jnp.where(r < 18, (r % 6) // 2, r - 18))
-            dy = jnp.where(r % 2 == 0, NY - k, k)
-            even = ((y + dy) % NY) % 2 == 0
+            return dz, jnp.where(r % 2 == 0, NY - k, k)
+
+        def q_dot(*blocks):
+            lhs = [xv[:, pl.ds(pl.multiple_of(b * BLK, BLK), BLK)] for b in blocks]
+            rhs = [wq[b] for b in blocks]
+            qacc[...] += jnp.dot(
+                jnp.concatenate(lhs, axis=1), jnp.concatenate(rhs, axis=0), preferred_element_type=jnp.float32)
+
+        @pl.loop(0, NZ * NY)
+        def _(m):
+            dz, dy = place(m)
             left = qi(3, dz, dy)
             right = qi(1, dz, dy)
-            q_wait(left)
-
-            @pl.when(even)
-            def _():
-                q_copy(left, on(0, dx=1)).start()
-
-            q_wait(right)
-
-            @pl.when(jnp.logical_not(even))
-            def _():
-                q_copy(right, on(0, dx=3)).start()
-
-            @pl.when(m % 8 == 4)
-            def _():
-                q_dot(0, m // 8)
-
-        @pl.loop(0, 6)
-        def _(m):
-            q_dot(3 - 2 * (m % 2), m // 2)
-
-        @pl.loop(0, NZ)
-        def _(dz):
-            @pl.loop(0, NY)
-            def _(n):
-                q_wait(qi(2, dz, n))
-
-            q_dot(2, dz)
+
+            @pl.when(m >= 9)
+            def _():
+                crossing(left, right, ((zl + dz) % NZ + (y + dy) % NY) % 2 == 0)
+
+            @pl.when(jnp.logical_and(m < 9, dz > 0))
+            def _():
+                q_wait(left)
+                q_wait(right)
+
+            q_dot(qi(0, dz, dy), left, right)
+
+        @pl.loop(0, NZ * NY // 2)
+        def _(n):
+            pair = []
+            for m in (2 * n, 2 * n + 1):
+                dz, dy = place(m)
+                b = qi(2, dz, dy)
+                pl.when(jnp.logical_or(m >= 9, dz > 0))(functools.partial(q_wait, b))
+                pair.append(b)
+            q_dot(*pair)
 
         qown[...] = qacc[...].astype(jnp.bfloat16)
         for k in (2, 1, 3, 0):
@@ -235,7 +269,7 @@
             half = o_half(own_o)
             half[...] = wos[...]
 
-        pl.semaphore_wait(barrier, 17)
+        pl.semaphore_wait(barrier, 16)
 
         @pl.when(jnp.logical_not(collector))
         def _():
@@ -271,8 +305,16 @@
 
             @pl.when(collector)
             def _():
-                for k in (2, 1, 3):
+                for k in (1, 3):
                     o_copy(b, on(1, dx=k), b_send).start()
+
+            @pl.when(jnp.logical_and(behind == 1, i % 2 == 0))
+            def _():
+                o_copy(b, on(1, dx=1), b_send).start()
+
+            @pl.when(jnp.logical_and(behind == 3, i % 2 == 1))
+            def _():
+                o_copy(b, on(1, dx=3), b_send).start()
 
             spread(b)
             lanes(b)
@@ -332,17 +374,21 @@
             cols = qcat.at[:, pl.ds(pl.multiple_of(h * 2 * BLK, 2 * BLK), 2 * BLK)]
             copy(cols, cols, q_send.at[k], q_recv.at[h], on(0, dh=k)).wait_recv()
 
-        def whole_sum(j):
-            w = wo[pl.ds(j * NH, NH)].reshape(NH * 2 * BLK, BLK)
-            return jnp.dot(qcat[...], w, preferred_element_type=jnp.float32).astype(jnp.bfloat16)
-
-        @pl.loop(0, HALF)
-        def _(j):
-            pout[j] = whole_sum(j)
+        def pair_sum(j):
+            w = [wo[pl.ds((j + k) * NH, NH)].reshape(NH * 2 * BLK, BLK) for k in (0, 1)]
+            return jnp.dot(qcat[...], jnp.concatenate(w, axis=1), preferred_element_type=jnp.float32).astype(jnp.bfloat16)
+
+        @pl.loop(0, HALF // 2)
+        def _(n):
+            j = 2 * n
+            both = pair_sum(j)
+            pout[j] = both[:, :BLK]
+            pout[j + 1] = both[:, BLK:]
             p_copy(j, 0).start()
-
-        for j in range(HALF):
-            out_ref[:, j * BLK:(j + 1) * BLK] = whole_sum(HALF + j)
+            p_copy(j + 1, 0).start()
+
+        for j in range(0, HALF, 2):
+            out_ref[:, j * BLK:(j + 2) * BLK] = pair_sum(HALF + j)
 
         for j in range(HALF):
             p_copy(j, 0).wait_send()
@@ -351,7 +397,11 @@
 
         @pl.when(collector)
         def _():
-            sent(wo.at[pl.ds(0, 12)], b_send)
+            sent(wo.at[pl.ds(0, 8)], b_send)
+
+        @pl.when(behind % 2 == 1)
+        def _():
+            sent(wo.at[pl.ds(0, 2)], b_send)
 
         @pl.when(jnp.logical_not(collector))
         def _():

time: 70 us -> 67.2 us (0.960)
  Pallas kernels: 66.6 us -> 63.7 us
    pallas_call x1, Pallas kernels: 66.6 us -> 63.7 us  [per_device(): pl.pallas_call(kernel, out_shape=jax.ShapeDtypeStruct((rows, HALF * BLK),...]
where the time goes in v3:
time: 67.2 us; the launch traced here: 66.7 us
  Pallas kernels  63.7 us (95%)
  local copies, waits for them, and re-layouts  1.77 us (3%)
  between operations  1.3 us (2%)
    pallas_call x1, Pallas kernels, per_device(): pl.pallas_call(kernel, out_shape=jax.ShapeDtypeStruct((rows, HALF * BLK),...  63.7 us
    unnamed x1, local copies, waits for them, and re-layouts  1.77 us

profile of v3, /device:TPU:1, one launch (start us, length us, event | category | flops | bytes accessed | tf_op | source)
XLA Modules:
  0.0 66.7 jit_solution(13928543887117967404)
XLA Ops:
  1.3 63.7 %shard_map.55 = bf16[128,1536]{1,0:T(8,128)(2,1)} custom-call(bf16[128,12288]{1,0:T(8,128)(2,1)} %x_hbm.1, f32[128,128]{1,0:T(8,128)} %qw_hbm.1, s32[1,1]{1,0:T(1,128)S(6)} %copy.7.qe_ref, f32[128,128]{1,0:T(8,128)} %ow_hbm.1, s32[1,1]{1,0:T(1,128)S(6)} %copy.8.oe_ref), custom_call_target="tpu_custom_call" | custom-call | flops 805306368 | bytes 4194304 | tf_op jit(solution)/shard_map/pallas_call | solution.py:420
  65.0 1.8 %copy.9 = bf16[128,1536]{1,0:T(8,128)(2,1)} copy(bf16[128,1536]{1,0:T(8,128)(2,1)} %shard_map.55) | data formatting | bytes 786432

commit v4 on v3

--- a/solution.py
+++ b/solution.py
@@ -11,6 +11,7 @@
 NX, NY, NZ, NH = 4, 8, 3, 4
 BLK = 128
 HALF = NZ * NY // 2
+AHEAD = 7
 VMEM_LIMIT = 61 << 20
 
 
@@ -194,16 +195,15 @@
                 opposite(7)
                 lanes(0)
 
-            @pl.when(n == 8)
-            def _():
-                lanes(1)
-                lanes(7)
 
         @pl.loop(0, NZ)
         def _(dz):
             b = qi(0, dz, 4)
             q_wait(b)
             planes(b)
+
+        lanes(1)
+        lanes(7)
 
         own = q_half(own_q)
         copy(own, own, wq_send, wq_recv.at[own_q], on(1)).wait_recv()
@@ -333,10 +333,7 @@
             even = ((zl + dz) % NZ + h + (y + k)) % 2 == 0
             return oi(dz, NY - k, h), oi(dz, k, h), even
 
-        @pl.loop(0, 30)
-        def _(m):
-            r = m % 10
-            k = 1 + m // 10
+        def hop(r, k):
             left, right, even = ring(r, k)
             o_wait(left)
 
@@ -350,19 +347,28 @@
             def _():
                 o_copy(right, on(1, dy=7), wo_send).start()
 
-            @pl.when(r == 0)
-            def _():
+            return left, right
+
+        @pl.loop(0, 27)
+        def _(m):
+            @pl.when(jnp.logical_and(m % AHEAD == 0, m < 3 * AHEAD))
+            def _():
+                left, right = hop(0, 1 + m // AHEAD)
                 lanes(left)
                 lanes(right)
 
-        @pl.loop(0, 10)
+            @pl.when(m == 3 * AHEAD)
+            def _():
+                last, _, _ = ring(0, 4)
+                o_wait(last)
+                lanes(last)
+
+            hop(1 + m % 9, 1 + m // 9)
+
+        @pl.loop(1, 10)
         def _(r):
             last, _, _ = ring(r, 4)
             o_wait(last)
-
-            @pl.when(r == 0)
-            def _():
-                lanes(last)
 
         @pl.loop(0, NY)
         def _(n):

time: 67.2 us -> 67.3 us (level)
  no operation moved by 1% of the time
where the time goes in v4:
time: 67.3 us; the launch traced here: 67.1 us
  Pallas kernels  64 us (95%)
  local copies, waits for them, and re-layouts  1.77 us (3%)
  between operations  1.3 us (2%)
    pallas_call x1, Pallas kernels, per_device(): pl.pallas_call(kernel, out_shape=jax.ShapeDtypeStruct((rows, HALF * BLK),...  64 us
    unnamed x1, local copies, waits for them, and re-layouts  1.77 us

profile of v4, /device:TPU:1, one launch (start us, length us, event | category | flops | bytes accessed | tf_op | source)
XLA Modules:
  0.0 67.1 jit_solution(16893861363987038044)
XLA Ops:
  1.3 64.0 %shard_map.55 = bf16[128,1536]{1,0:T(8,128)(2,1)} custom-call(bf16[128,12288]{1,0:T(8,128)(2,1)} %x_hbm.1, f32[128,128]{1,0:T(8,128)} %qw_hbm.1, s32[1,1]{1,0:T(1,128)S(6)} %copy.7.qe_ref, f32[128,128]{1,0:T(8,128)} %ow_hbm.1, s32[1,1]{1,0:T(1,128)S(6)} %copy.8.oe_ref), custom_call_target="tpu_custom_call" | custom-call | flops 805306368 | bytes 4194304 | tf_op jit(solution)/shard_map/pallas_call | solution.py:426
  65.3 1.8 %copy.9 = bf16[128,1536]{1,0:T(8,128)(2,1)} copy(bf16[128,1536]{1,0:T(8,128)(2,1)} %shard_map.55) | data formatting | bytes 786432
